TPU v7x, 512 devices: a whole 4x8x8 slice. The times are simulated.
512 devices in a mesh: dp: 16 (over y, core), expert: 32 (over z, x).
Axes of the slice: x: 4, y: 8, z: 8, core: 2. Of those that a mesh axis runs over, the one named last changes fastest.
Arguments:
- stream_q: bfloat16 [4096, 4096], P('dp', 'expert'), may hold values from -6 to 6
- stream_k: bfloat16 [4096, 4096], P('dp', 'expert'), may hold values from -6 to 6
- stream_v: bfloat16 [4096, 4096], P('dp', 'expert'), may hold values from -6 to 6
- conv_taps: float32 [3, 3, 4096], P(None, None, 'expert'), may hold values from -14 to 14
- norm_gain: bfloat16 [4096], P('expert'), may hold values from 0.3984375 to 1.59375
- slot_token: int32 [16, 384], P('dp'), may hold values from 0 to 256, as said below
- expert_count: int32 [16, 2], P('dp'), may hold values from 0 to 256, as said below
- route_prob: float32 [4096], P('dp'), may hold values from 0.25 to 1
- w_proj: bfloat16 [4096, 2, 8192], P('dp', None, 'expert'), may hold values from -0.09375 to 0.09375
- grad_out: bfloat16 [4096, 8192], P('dp', 'expert'), may hold values from -0.75 to 0.75
Outputs:
- activation: bfloat16 [4096, 8192], P('dp', 'expert')
- weight_grad: float32 [4096, 2, 8192], P('dp', None, 'expert')
Inputs may be any that keep to these rules, and one draw needn't show every extreme that they name: `slot_token`: for each index of dp the slots hold its 256 local token numbers, each exactly once, grouped by expert in expert order; each group starts at a multiple of 128 and is padded with the value 256 up to a multiple of 128; all slots after the last group hold 256. `expert_count`: the size of each expert's group in slot_token, before padding; each row sums to 256.
All inputs are finite; a program needn't handle non-finite values.
Results may differ from a plain program's by a relative error of at most 0.023.
Values may be sent and summed in bfloat16 or wider, within the bound.
No kernel may reach another device: no remote copies, remote signals or barrier semaphores. Data moves between devices by JAX's collectives and lax.ppermute only.
A program may use at most 64 MiB of HBM per device.

v0:
```python
import jax
import jax.numpy as jnp
from jax import lax
from jax.sharding import PartitionSpec as P

D = 4096
BLOCK = 128
epsilon = 1e-06


def from_behind(value, axis, steps):
    count = lax.axis_size(axis)
    leading, last = (max(0, -steps), min(count, count - steps))
    return lax.ppermute(value, axis, [(source, source + steps) for source in range(leading, last)])


def block_owner(counts, num_blocks):
    padded = (counts + BLOCK - 1) // BLOCK * BLOCK
    ends = jnp.cumsum(padded)
    starts = jnp.arange(num_blocks, dtype=jnp.int32) * BLOCK
    owner = jnp.sum((starts[:, None] >= ends[None, :]).astype(jnp.int32), axis=1)
    return jnp.minimum(owner, counts.shape[0] - 1)


def on_device(
    stream_q,
    stream_k,
    stream_v,
    conv_taps,
    norm_gain,
    slot_token,
    expert_count,
    route_prob,
    w_proj,
    grad_out,
):
    stacked = jnp.stack([stream_q, stream_k, stream_v])
    before = from_behind(stacked[:, -2:, :], "dp", 1)
    extended = jnp.concatenate([before, stacked], axis=1).astype(jnp.float32)
    convolved = (
        conv_taps[:, 0, None, :] * extended[:, 2:]
        + conv_taps[:, 1, None, :] * extended[:, 1:-1]
        + conv_taps[:, 2, None, :] * extended[:, :-2]
    )
    mixed = (convolved[0] * convolved[1] * convolved[2]).astype(jnp.bfloat16)
    mixed_f = mixed.astype(jnp.float32)
    total = lax.psum(jnp.sum(mixed_f * mixed_f, axis=1), "expert")
    inv_rms = lax.rsqrt(total / D + epsilon)
    normed = (mixed_f * inv_rms[:, None] * norm_gain.astype(jnp.float32)).astype(jnp.bfloat16)
    gathered = lax.all_gather(normed, "expert", axis=1, tiled=True)
    tok_count = gathered.shape[0]
    slots = slot_token[0]
    num_blocks = slots.shape[0] // BLOCK
    owner = block_owner(expert_count[0], num_blocks)
    padded_rows = jnp.concatenate(
        [gathered, jnp.zeros((1, gathered.shape[1]), jnp.bfloat16)], axis=0
    )
    x_blocks = padded_rows[slots].reshape(num_blocks, BLOCK, gathered.shape[1])
    hid_local = w_proj.shape[2]
    experts_here = w_proj.shape[1]
    selector = (owner[:, None] == jnp.arange(experts_here, dtype=jnp.int32)[None, :]).astype(
        jnp.bfloat16
    )
    columns = x_blocks
    chosen_w = jnp.einsum(
        "neh,be->bnh",
        lax.all_gather(w_proj, "dp", axis=0, tiled=True),
        selector,
        preferred_element_type=jnp.float32,
    ).astype(jnp.bfloat16)
    pre_act = jnp.einsum("brn,bnh->brh", columns, chosen_w, preferred_element_type=jnp.float32)
    pre_act = pre_act.reshape(num_blocks * BLOCK, hid_local)
    slot_prob = jnp.concatenate([route_prob, jnp.zeros((1,), jnp.float32)])[slots][:, None]
    sigmoid_z = jax.nn.sigmoid(pre_act)
    hidden = (slot_prob * pre_act * sigmoid_z).astype(jnp.bfloat16)
    activation = (
        jnp.zeros((tok_count + 1, hid_local), jnp.bfloat16).at[slots].set(hidden)[:tok_count]
    )
    slot_grad = jnp.concatenate([grad_out, jnp.zeros((1, hid_local), jnp.bfloat16)], axis=0)[
        slots
    ].astype(jnp.float32)
    grad_pre = (slot_grad * slot_prob * sigmoid_z * (1.0 + pre_act * (1.0 - sigmoid_z))).astype(
        jnp.bfloat16
    )
    grad_blocks = grad_pre.reshape(num_blocks, BLOCK, hid_local)
    masked_grad = grad_blocks[None, :, :, :] * selector.T[:, :, None, None]
    columns = x_blocks
    weight_grad = lax.psum_scatter(
        jnp.einsum(
            "brd,ebrh->deh", columns, masked_grad, preferred_element_type=jnp.float32
        ).astype(jnp.bfloat16),
        "dp",
        scatter_dimension=0,
        tiled=True,
    ).astype(jnp.float32)
    return (activation, weight_grad)


def solution(mesh):
    placed = (
        P("dp", "expert"),
        P("dp", "expert"),
        P("dp", "expert"),
        P(None, None, "expert"),
        P("expert"),
        P("dp", None),
        P("dp", None),
        P("dp"),
        P("dp", None, "expert"),
        P("dp", "expert"),
    )
    return jax.shard_map(
        on_device,
        mesh=mesh,
        in_specs=placed,
        out_specs=(P("dp", "expert"), P("dp", None, "expert")),
        check_vma=False,
    )
```

profile of v0, /device:TPU:29, one launch (start us, length us, event | category | flops | bytes accessed | tf_op | source)
XLA Modules:
  0.0 303.6 jit_solution(1994741817525698117)
XLA Ops:
  7.2 0.7 pad_maximum_fusion.1
  8.0 5.0 %collective-permute-start = (bf16[3,2,128]{2,1,0:T(2,128)(2,1)S(1)}, bf16[3,2,128]{2,1,0:T(2,128)(2,1)S(1)}, u32[]{:S(2)}, u32[]{:S(2)}) collective-permute-start(bf16[3,2,128]{2,1,0:T(2,128)(2,1)S(1)} %pad_maximum_fusion.1), channel_id=1, source_target_pairs={{0,32},{32,64},{64,96},{96,128},{128,160},{160,192},{192,224},{224... | collective-permute-start | bytes 4616 | tf_op jit(solution)/shard_map/ppermute | solution.py:14
  12.9 0.8 fusion.29
  13.8 0.7 convert_element_type.59
  14.4 0.9 maximum_convert_fusion
  15.6 62.6 %psum.7 = f32[256]{0:T(256)S(1)} all-reduce(f32[256]{0:T(256)S(1)} %get-tuple-element.10), channel_id=1, replica_groups=mesh['dp'=16,'expert'=32] {'expert'}, use_global_device_ids=true, to_apply=%region_1.0 | all-reduce | flops 256 | bytes 2048 | tf_op jit(solution)/shard_map/psum | solution.py:47
  78.2 0.7 fusion.17
  79.0 0.7 all-gather.5.cloned.1.call-update
  79.8 0.7 pad_maximum_fusion
  80.5 0.7 fusion.24
  81.2 2.8 gather_fusion
  84.0 2.6 gather_fusion.2
  86.6 0.2 reduce-window.8
  86.9 81.5 %all-gather.3.cloned.1.call-done = bf16[256,4096]{1,0:T(8,128)(2,1)} async-done(((bf16[256,128]{1,0:T(8,128)(2,1)}), bf16[256,4096]{1,0:T(8,128)(2,1)}) %all-gather.3.cloned.1.call-update) | async-done | bytes 2097168 | tf_op jit(solution)/shard_map/all_gather | solution.py:50
  168.4 1.8 concatenate.14
  170.1 4.1 %gather_fusion.1 = bf16[384,4096]{1,0:T(8,128)(2,1)} fusion(bf16[257,4096]{1,0:T(8,128)(2,1)S(1)} %concatenate.14, s32[1024]{0:T(1024)S(1)} %pad_clamp_fusion), kind=kCustom, calls=%fused_computation.1 | custom fusion | bytes 6292992 | tf_op jit(solution)/shard_map/gather | solution.py:58
  174.2 42.7 %all-gather.5.cloned.1.call-done = bf16[4096,2,256]{2,1,0:T(2,128)(2,1)} async-done(((bf16[256,2,256]{2,1,0:T(2,128)(2,1)}), bf16[4096,2,256]{2,1,0:T(2,128)(2,1)}) %all-gather.5.cloned.1.call-update) | async-done | bytes 4194320 | tf_op jit(solution)/shard_map/all_gather | solution.py:67
  217.0 7.5 %convolution_convert_fusion = bf16[3,4096,256]{2,0,1:T(4,128)(2,1)S(1)} fusion(bf16[4096,2,256]{2,1,0:T(2,128)(2,1)} %all-gather.5.cloned.1.call-done, s32[3]{0:T(128)S(1)} %broadcast_minimum_fusion), kind=kOutput, calls=%fused_computation.5 | convolution fusion | flops 15728646 | bytes 10485772 | tf_op jit(solution)/shard_map/neh,be->bnh/dot_general | solution.py:65
  224.5 1.3 fusion.6
  225.8 4.4 %bitcast_convert_fusion = bf16[4096,2,256]{2,0,1:T(8,128)(2,1)} fusion(bf16[3,128,4096,1]{2,1,0,3:T(8,128)(2,1)S(1)} %bitcast.50, bf16[2,3]{1,0:T(2,128)(2,1)S(1)} %compare_convert_fusion, bf16[3,128,256]{2,1,0:T(8,128)(2,1)S(1)} %get-tuple-element.15), kind=kOutput, calls=%fused_computation.4 | convolution fusion | flops 1613496320 | bytes 7536652 | tf_op jit(solution)/shard_map/brd,ebrh->deh/dot_general | solution.py:89
  230.3 1.9 scatter_custom_fusion
  232.2 0.7 slice.56
  232.8 62.2 %reduce-scatter.2.cloned.1.call-done = bf16[256,2,256]{2,0,1:T(8,128)(2,1)} async-done(((bf16[4096,2,256]{2,0,1:T(8,128)(2,1)}), bf16[256,2,256]{2,0,1:T(8,128)(2,1)}) %reduce-scatter.2.cloned.1.call-update) | async-done | bytes 262160 | tf_op jit(solution)/shard_map/reduce_scatter | solution.py:88
  295.1 2.0 copy.21
  (27 shorter events, 0.7 us)
Async XLA Ops:
  7.2 76.8 %copy-start.2 = (bf16[256,256]{1,0:T(8,128)(2,1)S(1)}, bf16[256,256]{1,0:T(8,128)(2,1)}, u32[]{:S(2)}) copy-start(bf16[256,256]{1,0:T(8,128)(2,1)} %param.19) | copy-start | bytes 393220
  7.2 79.4 %copy-start.3 = (s32[1,2]{1,0:T(1,128)S(1)}, s32[1,2]{1,0:T(1,128)}, u32[]{:S(2)}) copy-start(s32[1,2]{1,0:T(1,128)} %param.16) | copy-start | bytes 28
  7.2 161.2 %all-gather.3.cloned.1.call-start = ((), (), s32[]{:S(2)}) async-start(), calls=%async_computation.1 | async-start | bytes 2162688 | tf_op jit(solution)/shard_map/all_gather | solution.py:50
  8.0 6.5 %collective-permute-start = (bf16[3,2,128]{2,1,0:T(2,128)(2,1)S(1)}, bf16[3,2,128]{2,1,0:T(2,128)(2,1)S(1)}, u32[]{:S(2)}, u32[]{:S(2)}) collective-permute-start(bf16[3,2,128]{2,1,0:T(2,128)(2,1)S(1)} %pad_maximum_fusion.1), channel_id=1, source_target_pairs={{0,32},{32,64},{64,96},{96,128},{128,160},{160,192},{192,224},{224... | collective-permute-start | bytes 4616 | tf_op jit(solution)/shard_map/ppermute | solution.py:14
  79.0 138.0 %all-gather.5.cloned.1.call-start = ((), (), s32[]{:S(2)}) async-start(), calls=%async_computation.2 | async-start | bytes 4456448 | tf_op jit(solution)/shard_map/all_gather | solution.py:67
  79.7 215.3 %reduce-scatter.2.cloned.1.call-start = ((), (), s32[]{:S(2)}) async-start(), calls=%async_computation.3 | async-start | bytes 4456448 | tf_op jit(solution)/shard_map/reduce_scatter | solution.py:88
  174.2 50.2 %copy-start = (bf16[384,4096]{1,0:T(8,128)(2,1)S(1)}, bf16[384,4096]{1,0:T(8,128)(2,1)}, u32[]{:S(2)}) copy-start(bf16[384,4096]{1,0:T(8,128)(2,1)} %gather_fusion.1) | copy-start | bytes 9437188
  217.0 7.5 %copy-start.1 = (bf16[384,256]{1,0:T(8,128)(2,1)S(1)}, bf16[384,256]{1,0:T(8,128)(2,1)}, u32[]{:S(2)}) copy-start(bf16[384,256]{1,0:T(8,128)(2,1)} %gather_fusion.2) | copy-start | bytes 589828
Sparse Core Ops, SparseCore 0:
  79.1 89.2 all-gather.2
  170.5 46.4 all-gather.4
  230.3 64.7 reduce-scatter.1
where the time goes:
time: 304 us
  waiting for transfers between devices  187 us (62%)
  blocking collectives  62.6 us (21%)
  local copies, waits for them, and re-layouts  16.6 us (5%)
  between operations  13.9 us (5%)
  matrix products  13.1 us (4%)
  other arithmetic  5.15 us (2%)
  starting transfers between devices  5.08 us (2%)
    all_gather x1, waiting for transfers between devices, on_device(): gathered = lax.all_gather(normed, 'expert', axis=1, tiled=True)  81.5 us
    psum x1, blocking collectives, on_device(): total = lax.psum(jnp.sum(mixed_f * mixed_f, axis=1), 'expert')  62.6 us
    reduce_scatter x1, waiting for transfers between devices, on_device(): lax.psum_scatter(jnp.einsum('brd,ebrh->deh', columns, masked_grad, prefer...  62.2 us
    all_gather x1, waiting for transfers between devices, on_device(): lax.all_gather(w_proj, 'dp', axis=0, tiled=True)  42.7 us
    dot_general x1, matrix products, on_device(): jnp.einsum('neh,be->bnh', lax.all_gather(w_proj, 'dp', axis=0, tiled=True...  7.48 us
  transfers between devices with their start and end apart: 4, of which 3 were waited for; matrix products, arithmetic and copies ran while one was open for 6% of the time, Pallas kernels for 0%

commit v1 on v0

--- a/solution.py
+++ b/solution.py
@@ -6,6 +6,29 @@
 D = 4096
 BLOCK = 128
 epsilon = 1e-06
+
+
+def obtain_the_records(tile_in, body):
+    mesh_ax = "dp"
+    f_next = lax.axis_size(mesh_ax)
+    even = lax.axis_index(mesh_ax)
+    all_values, carry_in, oldest = (f_next, even, tile_in.shape[0])
+    value_now, front = ([], [])
+    carry_out = row_out = tile_in
+    for hop_no in range(all_values // 2 + 1):
+        value_now.append(body(carry_out, (carry_in - hop_no) % all_values * oldest))
+        if 0 < hop_no < all_values - all_values // 2:
+            front.append(body(row_out, (carry_in + hop_no) % all_values * oldest))
+        panels = []
+        for t in range(all_values):
+            panels.append((t, (t + 1) % all_values))
+        carry_out = lax.ppermute(carry_out, axis_name=mesh_ax, perm=panels)
+        sheets = []
+        for t in range(all_values):
+            sheets.append((t, (t - 1) % all_values))
+        row_out = lax.ppermute(row_out, axis_name=mesh_ax, perm=sheets)
+    w_next = jnp.concatenate([*value_now[::-1], *front], 1)
+    return jnp.roll(w_next, (carry_in - all_values // 2) * value_now[0].shape[1], 1)
 
 
 def from_behind(value, axis, steps):
@@ -62,11 +85,11 @@
         jnp.bfloat16
     )
     columns = x_blocks
-    chosen_w = jnp.einsum(
-        "neh,be->bnh",
-        lax.all_gather(w_proj, "dp", axis=0, tiled=True),
-        selector,
-        preferred_element_type=jnp.float32,
+    chosen_w = obtain_the_records(
+        w_proj,
+        lambda own_block, offset: jnp.einsum(
+            "neh,be->bnh", own_block, selector, preferred_element_type=jnp.float32
+        ),
     ).astype(jnp.bfloat16)
     pre_act = jnp.einsum("brn,bnh->brh", columns, chosen_w, preferred_element_type=jnp.float32)
     pre_act = pre_act.reshape(num_blocks * BLOCK, hid_local)

time: 304 us -> 272 us (0.89)
  the two profiles are of different devices: /device:TPU:29 before, /device:TPU:25 now
where the time goes in v1:
time: 272 us
  waiting for transfers between devices  77.2 us (28%)
  blocking collectives  66.9 us (25%)
  starting transfers between devices  44.4 us (16%)
  local copies, waits for them, and re-layouts  43.1 us (16%)
  matrix products  20.3 us (7%)
  between operations  14.4 us (5%)
  other arithmetic  5.79 us (2%)
    psum x1, blocking collectives, on_device(): total = lax.psum(jnp.sum(mixed_f * mixed_f, axis=1), 'expert')  66.9 us
    reduce_scatter x1, waiting for transfers between devices, on_device(): lax.psum_scatter(jnp.einsum('brd,ebrh->deh', columns, masked_grad, prefer...  61.3 us
    ppermute x8, starting transfers between devices, obtain_the_records(): carry_out = lax.ppermute(carry_out, axis_name=mesh_ax, perm=panels)  39.2 us
    unnamed x34, local copies, waits for them, and re-layouts  27.1 us
    ppermute x8, waiting for transfers between devices, obtain_the_records(): carry_out = lax.ppermute(carry_out, axis_name=mesh_ax, perm=panels)  15.3 us
    dot_general x16, matrix products, on_device(): jnp.einsum('neh,be->bnh', own_block, selector, preferred_element_type=jnp...  9.22 us
    dot_general x1, matrix products, on_device(): jnp.einsum('brd,ebrh->deh', columns, masked_grad, preferred_element_type=...  6.29 us
  transfers between devices with their start and end apart: 18, of which 11 were waited for; matrix products, arithmetic and copies ran while one was open for 18% of the time, Pallas kernels for 0%

profile of v1, /device:TPU:25, one launch (start us, length us, event | category | flops | bytes accessed | tf_op | source)
XLA Modules:
  0.0 272.0 jit_solution(12949090356885046290)
XLA Ops:
  7.2 3.1 %collective-permute-start.1 = (bf16[256,2,256]{2,1,0:T(2,128)(2,1)}, bf16[256,2,256]{2,1,0:T(2,128)(2,1)S(1)}, u32[]{:S(2)}, u32[]{:S(2)}) collective-permute-start(bf16[256,2,256]{2,1,0:T(2,128)(2,1)} %param.18), channel_id=1, source_target_pairs={{0,32},{32,64},{64,96},{96,128},{128,160},{160,192},{192,224},{224... | collective-permute-start | bytes 786440 | tf_op jit(solution)/shard_map/ppermute | solution.py:25
  11.0 4.8 %collective-permute-start = (bf16[3,2,128]{2,1,0:T(2,128)(2,1)S(1)}, bf16[3,2,128]{2,1,0:T(2,128)(2,1)S(1)}, u32[]{:S(2)}, u32[]{:S(2)}) collective-permute-start(bf16[3,2,128]{2,1,0:T(2,128)(2,1)S(1)} %pad_maximum_fusion.1), channel_id=1, source_target_pairs={{0,32},{32,64},{64,96},{96,128},{128,160},{160,192},{192,224},{224... | collective-permute-start | bytes 4616 | tf_op jit(solution)/shard_map/ppermute | solution.py:37
  21.2 2.8 %gather_fusion = f32[384]{0:T(512)S(1)} fusion(f32[257]{0:T(512)S(1)} %pad_maximum_fusion, s32[1024]{0:T(1024)S(1)} %pad_clamp_fusion), kind=kCustom, calls=%fused_computation | custom fusion | bytes 4608 | tf_op jit(solution)/shard_map/gather | solution.py:96
  24.9 2.1 gather_fusion.2
  28.2 66.9 %psum.7 = f32[256]{0:T(256)S(1)} all-reduce(f32[256]{0:T(256)S(1)} %get-tuple-element.10), channel_id=1, replica_groups=mesh['dp'=16,'expert'=32] {'expert'}, use_global_device_ids=true, to_apply=%region_1.0 | all-reduce | flops 256 | bytes 2048 | tf_op jit(solution)/shard_map/psum | solution.py:70
  96.1 14.0 %collective-permute-start.2 = (bf16[256,2,256]{2,1,0:T(2,128)(2,1)S(1)}, bf16[256,2,256]{2,1,0:T(2,128)(2,1)S(1)}, u32[]{:S(2)}, u32[]{:S(2)}) collective-permute-start(bf16[256,2,256]{2,1,0:T(2,128)(2,1)S(1)} %collective-permute-done.1), channel_id=1, source_target_pairs={{0,32},{32,64},{64,96},{96,128},{128,160},{160,192},{192,224},{224... | collective-permute-start | bytes 786440 | tf_op jit(solution)/shard_map/ppermute | solution.py:25
  111.2 2.2 collective-permute-done.2
  113.4 3.7 %collective-permute-start.3 = (bf16[256,2,256]{2,1,0:T(2,128)(2,1)S(1)}, bf16[256,2,256]{2,1,0:T(2,128)(2,1)S(1)}, u32[]{:S(2)}, u32[]{:S(2)}) collective-permute-start(bf16[256,2,256]{2,1,0:T(2,128)(2,1)S(1)} %collective-permute-done.2), channel_id=1, source_target_pairs={{0,32},{32,64},{64,96},{96,128},{128,160},{160,192},{192,224},{224... | collective-permute-start | bytes 786440 | tf_op jit(solution)/shard_map/ppermute | solution.py:25
  118.2 2.2 collective-permute-done.3
  120.4 3.7 %collective-permute-start.4 = (bf16[256,2,256]{2,1,0:T(2,128)(2,1)S(1)}, bf16[256,2,256]{2,1,0:T(2,128)(2,1)S(1)}, u32[]{:S(2)}, u32[]{:S(2)}) collective-permute-start(bf16[256,2,256]{2,1,0:T(2,128)(2,1)S(1)} %collective-permute-done.3), channel_id=1, source_target_pairs={{0,32},{32,64},{64,96},{96,128},{128,160},{160,192},{192,224},{224... | collective-permute-start | bytes 786440 | tf_op jit(solution)/shard_map/ppermute | solution.py:25
  125.2 2.2 collective-permute-done.4
  127.4 3.7 %collective-permute-start.5 = (bf16[256,2,256]{2,1,0:T(2,128)(2,1)S(1)}, bf16[256,2,256]{2,1,0:T(2,128)(2,1)S(1)}, u32[]{:S(2)}, u32[]{:S(2)}) collective-permute-start(bf16[256,2,256]{2,1,0:T(2,128)(2,1)S(1)} %collective-permute-done.4), channel_id=1, source_target_pairs={{0,32},{32,64},{64,96},{96,128},{128,160},{160,192},{192,224},{224... | collective-permute-start | bytes 786440 | tf_op jit(solution)/shard_map/ppermute | solution.py:25
  132.2 2.2 collective-permute-done.5
  134.4 3.7 %collective-permute-start.6 = (bf16[256,2,256]{2,1,0:T(2,128)(2,1)S(1)}, bf16[256,2,256]{2,1,0:T(2,128)(2,1)S(1)}, u32[]{:S(2)}, u32[]{:S(2)}) collective-permute-start(bf16[256,2,256]{2,1,0:T(2,128)(2,1)S(1)} %collective-permute-done.5), channel_id=1, source_target_pairs={{0,32},{32,64},{64,96},{96,128},{128,160},{160,192},{192,224},{224... | collective-permute-start | bytes 786440 | tf_op jit(solution)/shard_map/ppermute | solution.py:25
  139.3 2.1 collective-permute-done.6
  141.4 3.7 %collective-permute-start.7 = (bf16[256,2,256]{2,1,0:T(2,128)(2,1)S(1)}, bf16[256,2,256]{2,1,0:T(2,128)(2,1)S(1)}, u32[]{:S(2)}, u32[]{:S(2)}) collective-permute-start(bf16[256,2,256]{2,1,0:T(2,128)(2,1)S(1)} %collective-permute-done.6), channel_id=1, source_target_pairs={{0,32},{32,64},{64,96},{96,128},{128,160},{160,192},{192,224},{224... | collective-permute-start | bytes 786440 | tf_op jit(solution)/shard_map/ppermute | solution.py:25
  146.3 2.1 collective-permute-done.7
  148.4 3.7 %collective-permute-start.8 = (bf16[256,2,256]{2,1,0:T(2,128)(2,1)S(1)}, bf16[256,2,256]{2,1,0:T(2,128)(2,1)S(1)}, u32[]{:S(2)}, u32[]{:S(2)}) collective-permute-start(bf16[256,2,256]{2,1,0:T(2,128)(2,1)S(1)} %collective-permute-done.7), channel_id=1, source_target_pairs={{0,32},{32,64},{64,96},{96,128},{128,160},{160,192},{192,224},{224... | collective-permute-start | bytes 786440 | tf_op jit(solution)/shard_map/ppermute | solution.py:25
  153.3 2.1 collective-permute-done.8
  183.7 4.3 %gather_fusion.1 = bf16[384,4096]{1,0:T(8,128)(2,1)} fusion(bf16[257,4096]{1,0:T(8,128)(2,1)S(1)} %concatenate.20, s32[1024]{0:T(1024)S(1)} %pad_clamp_fusion), kind=kCustom, calls=%fused_computation.1 | custom fusion | bytes 6292992 | tf_op jit(solution)/shard_map/gather | solution.py:81
  187.9 4.8 %fusion.5 = (bf16[3,128,256]{2,1,0:T(8,128)(2,1)S(1)}, f32[3,128,256]{2,1,0:T(8,128)S(1)}) fusion(bf16[3,128,256]{2,1,0:T(8,128)(2,1)S(1)} %bitcast.102, f32[3,128]{1,0:T(4,128)S(1)} %bitcast.104, bf16[3,128,4096]{2,1,0:T(8,128)(2,1)} %bitcast.94, bf16[3,8192,256]{2,1,0:T(8,128)(2,1)} %copy_dynamic-update-slice_fusion.1, s32[]{:T(128)S(6)} %select_n.38), kind=kOutput, calls=%fused_computation.47 | convolution fusion | flops 806387712 | bytes 10225156 | tf_op jit(solution)/shard_map/brn,bnh->brh/dot_general | solution.py:94
  192.8 6.3 %bitcast_convert_fusion = bf16[4096,2,256]{2,0,1:T(8,128)(2,1)} fusion(bf16[3,128,4096,1]{2,1,0,3:T(8,128)(2,1)} %bitcast.95, bf16[2,3]{1,0:T(2,128)(2,1)S(1)} %compare_convert_fusion, bf16[3,128,256]{2,1,0:T(8,128)(2,1)S(1)} %get-tuple-element.15), kind=kOutput, calls=%fused_computation.5 | convolution fusion | flops 1613496320 | bytes 7536652 | tf_op jit(solution)/shard_map/brd,ebrh->deh/dot_general | solution.py:112
  201.8 61.3 %reduce-scatter.2.cloned.1.call-done = bf16[256,2,256]{2,0,1:T(8,128)(2,1)} async-done(((bf16[4096,2,256]{2,0,1:T(8,128)(2,1)}), bf16[256,2,256]{2,0,1:T(8,128)(2,1)}) %reduce-scatter.2.cloned.1.call-update) | async-done | bytes 262160 | tf_op jit(solution)/shard_map/reduce_scatter | solution.py:111
  263.1 2.0 copy.52
  (93 shorter events, 47.7 us)
Async XLA Ops:
  7.2 174.7 %all-gather.2.cloned.1.call-start = ((), (), s32[]{:S(2)}) async-start(), calls=%async_computation.1 | async-start | bytes 2162688 | tf_op jit(solution)/shard_map/all_gather | solution.py:73
  7.2 88.9 %collective-permute-start.1 = (bf16[256,2,256]{2,1,0:T(2,128)(2,1)}, bf16[256,2,256]{2,1,0:T(2,128)(2,1)S(1)}, u32[]{:S(2)}, u32[]{:S(2)}) collective-permute-start(bf16[256,2,256]{2,1,0:T(2,128)(2,1)} %param.18), channel_id=1, source_target_pairs={{0,32},{32,64},{64,96},{96,128},{128,160},{160,192},{192,224},{224... | collective-permute-start | bytes 786440 | tf_op jit(solution)/shard_map/ppermute | solution.py:25
  10.3 100.3 %collective-permute-start.9 = (bf16[256,2,256]{2,1,0:T(2,128)(2,1)}, bf16[256,2,256]{2,1,0:T(2,128)(2,1)S(1)}, u32[]{:S(2)}, u32[]{:S(2)}) collective-permute-start(bf16[256,2,256]{2,1,0:T(2,128)(2,1)} %param.18), channel_id=1, source_target_pairs={{0,480},{32,0},{64,32},{96,64},{128,96},{160,128},{192,160},{224,1... | collective-permute-start | bytes 786440 | tf_op jit(solution)/shard_map/ppermute | solution.py:29
  11.0 16.0 %collective-permute-start = (bf16[3,2,128]{2,1,0:T(2,128)(2,1)S(1)}, bf16[3,2,128]{2,1,0:T(2,128)(2,1)S(1)}, u32[]{:S(2)}, u32[]{:S(2)}) collective-permute-start(bf16[3,2,128]{2,1,0:T(2,128)(2,1)S(1)} %pad_maximum_fusion.1), channel_id=1, source_target_pairs={{0,32},{32,64},{64,96},{96,128},{128,160},{160,192},{192,224},{224... | collective-permute-start | bytes 4616 | tf_op jit(solution)/shard_map/ppermute | solution.py:37
  95.9 167.3 %reduce-scatter.2.cloned.1.call-start = ((), (), s32[]{:S(2)}) async-start(), calls=%async_computation.2 | async-start | bytes 4456448 | tf_op jit(solution)/shard_map/reduce_scatter | solution.py:111
  96.1 17.3 %collective-permute-start.2 = (bf16[256,2,256]{2,1,0:T(2,128)(2,1)S(1)}, bf16[256,2,256]{2,1,0:T(2,128)(2,1)S(1)}, u32[]{:S(2)}, u32[]{:S(2)}) collective-permute-start(bf16[256,2,256]{2,1,0:T(2,128)(2,1)S(1)} %collective-permute-done.1), channel_id=1, source_target_pairs={{0,32},{32,64},{64,96},{96,128},{128,160},{160,192},{192,224},{224... | collective-permute-start | bytes 786440 | tf_op jit(solution)/shard_map/ppermute | solution.py:25
  110.6 7.0 %collective-permute-start.10 = (bf16[256,2,256]{2,1,0:T(2,128)(2,1)S(1)}, bf16[256,2,256]{2,1,0:T(2,128)(2,1)S(1)}, u32[]{:S(2)}, u32[]{:S(2)}) collective-permute-start(bf16[256,2,256]{2,1,0:T(2,128)(2,1)S(1)} %collective-permute-done.9), channel_id=1, source_target_pairs={{0,480},{32,0},{64,32},{96,64},{128,96},{160,128},{192,160},{224,1... | collective-permute-start | bytes 786440 | tf_op jit(solution)/shard_map/ppermute | solution.py:29
  113.4 7.0 %collective-permute-start.3 = (bf16[256,2,256]{2,1,0:T(2,128)(2,1)S(1)}, bf16[256,2,256]{2,1,0:T(2,128)(2,1)S(1)}, u32[]{:S(2)}, u32[]{:S(2)}) collective-permute-start(bf16[256,2,256]{2,1,0:T(2,128)(2,1)S(1)} %collective-permute-done.2), channel_id=1, source_target_pairs={{0,32},{32,64},{64,96},{96,128},{128,160},{160,192},{192,224},{224... | collective-permute-start | bytes 786440 | tf_op jit(solution)/shard_map/ppermute | solution.py:25
  117.6 7.0 %collective-permute-start.11 = (bf16[256,2,256]{2,1,0:T(2,128)(2,1)S(1)}, bf16[256,2,256]{2,1,0:T(2,128)(2,1)S(1)}, u32[]{:S(2)}, u32[]{:S(2)}) collective-permute-start(bf16[256,2,256]{2,1,0:T(2,128)(2,1)S(1)} %collective-permute-done.10), channel_id=1, source_target_pairs={{0,480},{32,0},{64,32},{96,64},{128,96},{160,128},{192,160},{224,1... | collective-permute-start | bytes 786440 | tf_op jit(solution)/shard_map/ppermute | solution.py:29
  120.4 7.0 %collective-permute-start.4 = (bf16[256,2,256]{2,1,0:T(2,128)(2,1)S(1)}, bf16[256,2,256]{2,1,0:T(2,128)(2,1)S(1)}, u32[]{:S(2)}, u32[]{:S(2)}) collective-permute-start(bf16[256,2,256]{2,1,0:T(2,128)(2,1)S(1)} %collective-permute-done.3), channel_id=1, source_target_pairs={{0,32},{32,64},{64,96},{96,128},{128,160},{160,192},{192,224},{224... | collective-permute-start | bytes 786440 | tf_op jit(solution)/shard_map/ppermute | solution.py:25
  124.7 7.0 %collective-permute-start.12 = (bf16[256,2,256]{2,1,0:T(2,128)(2,1)S(1)}, bf16[256,2,256]{2,1,0:T(2,128)(2,1)S(1)}, u32[]{:S(2)}, u32[]{:S(2)}) collective-permute-start(bf16[256,2,256]{2,1,0:T(2,128)(2,1)S(1)} %collective-permute-done.11), channel_id=1, source_target_pairs={{0,480},{32,0},{64,32},{96,64},{128,96},{160,128},{192,160},{224,1... | collective-permute-start | bytes 786440 | tf_op jit(solution)/shard_map/ppermute | solution.py:29
  127.4 7.0 %collective-permute-start.5 = (bf16[256,2,256]{2,1,0:T(2,128)(2,1)S(1)}, bf16[256,2,256]{2,1,0:T(2,128)(2,1)S(1)}, u32[]{:S(2)}, u32[]{:S(2)}) collective-permute-start(bf16[256,2,256]{2,1,0:T(2,128)(2,1)S(1)} %collective-permute-done.4), channel_id=1, source_target_pairs={{0,32},{32,64},{64,96},{96,128},{128,160},{160,192},{192,224},{224... | collective-permute-start | bytes 786440 | tf_op jit(solution)/shard_map/ppermute | solution.py:25
  131.7 7.1 %collective-permute-start.13 = (bf16[256,2,256]{2,1,0:T(2,128)(2,1)S(1)}, bf16[256,2,256]{2,1,0:T(2,128)(2,1)S(1)}, u32[]{:S(2)}, u32[]{:S(2)}) collective-permute-start(bf16[256,2,256]{2,1,0:T(2,128)(2,1)S(1)} %collective-permute-done.12), channel_id=1, source_target_pairs={{0,480},{32,0},{64,32},{96,64},{128,96},{160,128},{192,160},{224,1... | collective-permute-start | bytes 786440 | tf_op jit(solution)/shard_map/ppermute | solution.py:29
  134.4 7.0 %collective-permute-start.6 = (bf16[256,2,256]{2,1,0:T(2,128)(2,1)S(1)}, bf16[256,2,256]{2,1,0:T(2,128)(2,1)S(1)}, u32[]{:S(2)}, u32[]{:S(2)}) collective-permute-start(bf16[256,2,256]{2,1,0:T(2,128)(2,1)S(1)} %collective-permute-done.5), channel_id=1, source_target_pairs={{0,32},{32,64},{64,96},{96,128},{128,160},{160,192},{192,224},{224... | collective-permute-start | bytes 786440 | tf_op jit(solution)/shard_map/ppermute | solution.py:25
  138.8 7.0 %collective-permute-start.14 = (bf16[256,2,256]{2,1,0:T(2,128)(2,1)S(1)}, bf16[256,2,256]{2,1,0:T(2,128)(2,1)S(1)}, u32[]{:S(2)}, u32[]{:S(2)}) collective-permute-start(bf16[256,2,256]{2,1,0:T(2,128)(2,1)S(1)} %collective-permute-done.13), channel_id=1, source_target_pairs={{0,480},{32,0},{64,32},{96,64},{128,96},{160,128},{192,160},{224,1... | collective-permute-start | bytes 786440 | tf_op jit(solution)/shard_map/ppermute | solution.py:29
  141.4 7.0 %collective-permute-start.7 = (bf16[256,2,256]{2,1,0:T(2,128)(2,1)S(1)}, bf16[256,2,256]{2,1,0:T(2,128)(2,1)S(1)}, u32[]{:S(2)}, u32[]{:S(2)}) collective-permute-start(bf16[256,2,256]{2,1,0:T(2,128)(2,1)S(1)} %collective-permute-done.6), channel_id=1, source_target_pairs={{0,32},{32,64},{64,96},{96,128},{128,160},{160,192},{192,224},{224... | collective-permute-start | bytes 786440 | tf_op jit(solution)/shard_map/ppermute | solution.py:25
  145.8 7.0 %collective-permute-start.15 = (bf16[256,2,256]{2,1,0:T(2,128)(2,1)S(1)}, bf16[256,2,256]{2,1,0:T(2,128)(2,1)S(1)}, u32[]{:S(2)}, u32[]{:S(2)}) collective-permute-start(bf16[256,2,256]{2,1,0:T(2,128)(2,1)S(1)} %collective-permute-done.14), channel_id=1, source_target_pairs={{0,480},{32,0},{64,32},{96,64},{128,96},{160,128},{192,160},{224,1... | collective-permute-start | bytes 786440 | tf_op jit(solution)/shard_map/ppermute | solution.py:29
  148.4 7.0 %collective-permute-start.8 = (bf16[256,2,256]{2,1,0:T(2,128)(2,1)S(1)}, bf16[256,2,256]{2,1,0:T(2,128)(2,1)S(1)}, u32[]{:S(2)}, u32[]{:S(2)}) collective-permute-start(bf16[256,2,256]{2,1,0:T(2,128)(2,1)S(1)} %collective-permute-done.7), channel_id=1, source_target_pairs={{0,32},{32,64},{64,96},{96,128},{128,160},{160,192},{192,224},{224... | collective-permute-start | bytes 786440 | tf_op jit(solution)/shard_map/ppermute | solution.py:25
Sparse Core Ops, SparseCore 0:
  96.0 82.1 all-gather.1
  199.2 63.8 reduce-scatter.1
